TPU v7x, 512 devices: a whole 4x8x8 slice. The times are simulated.
512 devices in a mesh: dp: 4 (over z_hi), segment: 16 (over y, core), patch: 8 (over x, z_lo).
Axes of the slice: x: 4, y: 8, z: 8 (z_hi: 4, z_lo: 2; z = z_hi * 2 + z_lo), core: 2. Of those that a mesh axis runs over, the one named last changes fastest.
Arguments:
- hidden: bfloat16 [64, 1024, 1536], P(('dp', 'segment'), 'patch'), parts along dimension 0, may hold values from -6 to 6
- w_qkv: bfloat16 [16, 1536, 4608], P('segment', None, 'patch'), may hold values from -0.12552947 to 0.12552947
- norm_gain: float32 [16, 1536], P('segment'), may hold values from 0.5 to 1.5
- box_vec: float32 [16, 1536], P('segment'), may hold values from -4 to 4
- gate: float32 [64, 1536], P(('dp', 'segment')), parts along dimension 0, may hold values from 4 to 16
- box_mask: int32 [64, 1024], P(('dp', 'segment'), 'patch'), parts along dimension 0, may hold values 0 or 1
- stale_kv: bfloat16 [64, 2, 1024, 1536], P(('dp', 'segment'), None, 'patch'), parts along dimension 0, may hold values from -6 to 6
Outputs:
- hidden_out: bfloat16 [64, 1024, 1536], P(('dp', 'segment'), 'patch'), parts along dimension 0
- fresh_kv: bfloat16 [64, 2, 1024, 1536], P(('dp', 'segment'), None, 'patch'), parts along dimension 0
There are 4 independent parts, one for each index of `dp`. A program takes and returns all parts, laid end to end along the dimension named above; an argument that names none is the same for every part. Nothing has to cross between parts.
All inputs are finite; a program needn't handle non-finite values. No bound on the sum of `box_mask` on one device may be relied on, other than what follows from the above.
Results may differ from a plain program's by a relative error of at most 0.023.
Values may be sent and summed in bfloat16 or wider, within the bound.
No kernel may reach another device: no remote copies, remote signals or barrier semaphores. Data moves between devices by JAX's collectives and lax.ppermute only.
A program may use at most 64 MiB of HBM per device.

v0:
```python
import jax
import jax.numpy as jnp
from jax import lax
from jax.sharding import PartitionSpec as P

HEADS = 12
HEAD_DIM = 128


def from_behind(shard, axis, by):
    count = lax.axis_size(axis)
    return lax.ppermute(shard, axis, [(i, (i + by) % count) for i in range(count)])


def partial_attention(queries, keys, values):
    count = queries.shape[0]
    length = keys.shape[0]
    qh = queries.reshape(count, HEADS, HEAD_DIM)
    kh = keys.reshape(length, HEADS, HEAD_DIM)
    vh = values.reshape(length, HEADS, HEAD_DIM)
    scores = jnp.einsum("nhd,thd->nht", qh, kh, preferred_element_type=jnp.float32) * HEAD_DIM ** (
        -0.5
    )
    top = jnp.max(scores, axis=-1)
    weights = jnp.exp(scores - top[..., None])
    total = jnp.sum(weights, axis=-1)
    summed = jnp.einsum(
        "nht,thd->nhd", weights.astype(jnp.bfloat16), vh, preferred_element_type=jnp.float32
    )
    return (summed.reshape(count, HEADS * HEAD_DIM), top, total)


def local(hidden, w_qkv, norm_gain, box_vec, gate, box_mask, stale_kv):
    state = hidden[0].astype(jnp.float32)
    rows = state.shape[0]
    width = HEADS * HEAD_DIM
    inverse = lax.rsqrt(jnp.mean(state * state, axis=-1, keepdims=True) + 1e-06)
    normed = (
        state * inverse * norm_gain[0] + box_mask[0][:, None].astype(jnp.float32) * box_vec[0]
    ).astype(jnp.bfloat16)
    weight = w_qkv[0]
    columns = jnp.dot(
        lax.all_gather(normed, "patch", axis=0, tiled=True),
        weight,
        preferred_element_type=jnp.float32,
    ).astype(jnp.bfloat16)
    qkv = lax.all_to_all(columns, "patch", split_axis=0, concat_axis=1, tiled=True)
    queries = qkv[:, :width]
    keys_new = qkv[:, width : 2 * width]
    values_new = qkv[:, 2 * width :]
    fresh = jnp.stack([keys_new, values_new])
    own_start = lax.axis_index("patch") * rows
    whole = lax.all_gather(stale_kv[0], "patch", axis=1, tiled=True)
    whole = lax.dynamic_update_slice_in_dim(whole, fresh, own_start, 1)
    summed, top, total = partial_attention(queries, whole[0], whole[1])
    attended = (summed.reshape(rows, HEADS, HEAD_DIM) / total[..., None]).reshape(rows, width)
    updated = (state + gate[0] * attended).astype(jnp.bfloat16)
    passed = from_behind(updated[None], "segment", 1)
    return (passed, fresh[None])


def solution(mesh):
    placed = (
        P(("dp", "segment"), "patch", None),
        P("segment", None, "patch"),
        P("segment", None),
        P("segment", None),
        P(("dp", "segment"), None),
        P(("dp", "segment"), "patch"),
        P(("dp", "segment"), None, "patch", None),
    )
    return jax.shard_map(
        local,
        mesh=mesh,
        in_specs=placed,
        out_specs=(P(("dp", "segment"), "patch", None), P(("dp", "segment"), None, "patch", None)),
        check_vma=False,
    )
```

profile of v0, /device:TPU:2, one launch (start us, length us, event | category | flops | bytes accessed | tf_op | source)
XLA Modules:
  0.0 266.6 jit_solution(11302217391138647032)
XLA Ops:
  7.2 0.0 copy-start
  7.2 0.0 all-gather.4.cloned.1.call-start
  7.2 0.8 reduce.1
  8.1 0.7 reduce.2
  8.8 1.2 fusion.23
  9.9 0.7 convert_bitcast_fusion.1
  10.6 2.0 fusion.26
  12.6 0.0 all-gather.4.cloned.1.call-update
  12.6 0.0 all-gather.6.cloned.1.call-start
  12.7 2.3 copy.13
  15.0 0.0 all-gather.6.cloned.1.call-update
  15.0 78.0 %all-gather.4.cloned.1.call-done = bf16[1024,1536]{1,0:T(8,128)(2,1)} async-done(((bf16[128,1536]{1,0:T(8,128)(2,1)}), bf16[1024,1536]{1,0:T(8,128)(2,1)}) %all-gather.4.cloned.1.call-update) | async-done | bytes 3145744 | tf_op jit(solution)/shard_map/all_gather | solution.py:43
  93.0 0.0 copy-done
  93.0 3.9 %fusion.12 = bf16[72,8,8,128]{3,2,1,0:T(8,128)(2,1)S(1)} fusion(bf16[1024,1536]{1,0:T(8,128)(2,1)} %all-gather.4.cloned.1.call-done, bf16[1,1536,576]{1,2,0:T(8,128)(2,1)S(1)} %copy-done), kind=kOutput, calls=%fused_computation.11 | convolution fusion | flops 1812529152 | bytes 6094848 | tf_op jit(solution)/shard_map/dot_general | solution.py:42
  96.9 0.0 copy-start.2
  96.9 1.3 copy.25
  98.2 5.4 %all-to-all-start = ((bf16[8,128,576]{1,2,0:T(8,128)(2,1)}), bf16[8,128,576]{1,2,0:T(8,128)(2,1)S(1)}, u32[]{:S(2)}, u32[]{:S(2)}) async-start(bf16[8,128,576]{1,2,0:T(8,128)(2,1)} %bitcast.67), calls=%async_computation | async-start | bytes 2359296 | tf_op jit(solution)/shard_map/all_to_all | solution.py:47
  103.5 0.0 copy-done.2
  103.5 21.3 %all-to-all-done = bf16[8,128,576]{1,2,0:T(8,128)(2,1)S(1)} async-done(((bf16[8,128,576]{1,2,0:T(8,128)(2,1)}), bf16[8,128,576]{1,2,0:T(8,128)(2,1)S(1)}, u32[]{:S(2)}, u32[]{:S(2)}) %all-to-all-start) | async-done | bytes 1179680 | tf_op jit(solution)/shard_map/all_to_all | solution.py:47
  124.9 1.0 fusion.32
  125.9 110.5 %all-gather.6.cloned.1.call-done = bf16[1,2,1024,1536]{2,3,1,0:T(8,128)(2,1)} async-done(((bf16[1,2,128,1536]{2,3,1,0:T(8,128)(2,1)}), bf16[1,2,1024,1536]{2,3,1,0:T(8,128)(2,1)}) %all-gather.6.cloned.1.call-update) | async-done | bytes 6291472 | tf_op jit(solution)/shard_map/all_gather | solution.py:53
  236.3 2.3 fusion.28
  238.7 3.6 %fusion.31 = (bf16[1,1024,1536]{1,2,0:T(8,128)(2,1)S(1)}, bf16[1,1024,1536]{1,2,0:T(8,128)(2,1)S(1)}) fusion(bf16[2,1024,1536]{1,2,0:T(8,128)(2,1)} %get-tuple-element.10), kind=kLoop, calls=%fused_computation.32 | loop fusion | bytes 12582912 | tf_op jit(solution)/shard_map/slice | solution.py:55
  242.2 1.3 bitcast_reduce_fusion
  243.5 1.0 fusion.1
  244.5 0.0 copy-start.1
  244.6 2.6 fusion.20
  247.1 2.3 copy.18
  249.4 0.0 copy-done.1
  249.4 1.2 fusion.27
  250.6 0.1 collective-permute-start
  250.7 1.2 copy.19
  251.9 7.2 %collective-permute-done = bf16[1,128,1536]{2,1,0:T(8,128)(2,1)S(1)} collective-permute-done((bf16[1,128,1536]{2,1,0:T(8,128)(2,1)S(1)}, bf16[1,128,1536]{2,1,0:T(8,128)(2,1)S(1)}, u32[]{:S(2)}, u32[]{:S(2)}) %collective-permute-start) | collective-permute-done | bytes 393248 | tf_op jit(solution)/shard_map/ppermute | solution.py:12
  259.1 0.7 copy.28
  (2 shorter events, 0.0 us)
Async XLA Ops:
  7.2 85.8 %copy-start = (bf16[1,1536,576]{1,2,0:T(8,128)(2,1)S(1)}, bf16[1,1536,576]{1,2,0:T(8,128)(2,1)}, u32[]{:S(2)}) copy-start(bf16[1,1536,576]{1,2,0:T(8,128)(2,1)} %param.8) | copy-start | bytes 5308420
  7.2 85.8 %all-gather.4.cloned.1.call-start = ((), (), s32[]{:S(2)}) async-start(), calls=%async_computation.1 | async-start | bytes 3538944 | tf_op jit(solution)/shard_map/all_gather | solution.py:43
  12.6 223.7 %all-gather.6.cloned.1.call-start = ((), (), s32[]{:S(2)}) async-start(), calls=%async_computation.2 | async-start | bytes 7077888 | tf_op jit(solution)/shard_map/all_gather | solution.py:53
  96.9 6.6 %copy-start.2 = (f32[1,1536]{1,0:T(1,128)S(1)}, f32[1,1536]{1,0:T(1,128)}, u32[]{:S(2)}) copy-start(f32[1,1536]{1,0:T(1,128)} %param.11) | copy-start | bytes 18436
  98.2 26.7 %all-to-all-start = ((bf16[8,128,576]{1,2,0:T(8,128)(2,1)}), bf16[8,128,576]{1,2,0:T(8,128)(2,1)S(1)}, u32[]{:S(2)}, u32[]{:S(2)}) async-start(bf16[8,128,576]{1,2,0:T(8,128)(2,1)} %bitcast.67), calls=%async_computation | async-start | bytes 2359296 | tf_op jit(solution)/shard_map/all_to_all | solution.py:47
  244.5 4.9 %copy-start.1 = (bf16[1,128,1536]{2,1,0:T(8,128)(2,1)S(1)}, bf16[1,128,1536]{2,1,0:T(8,128)(2,1)}, u32[]{:S(2)}) copy-start(bf16[1,128,1536]{2,1,0:T(8,128)(2,1)} %param.7) | copy-start | bytes 1179652
  250.6 8.4 %collective-permute-start = (bf16[1,128,1536]{2,1,0:T(8,128)(2,1)S(1)}, bf16[1,128,1536]{2,1,0:T(8,128)(2,1)S(1)}, u32[]{:S(2)}, u32[]{:S(2)}) collective-permute-start(bf16[1,128,1536]{2,1,0:T(8,128)(2,1)S(1)} %fusion.27), channel_id=1, source_target_pairs={{0,8},{8,16},{16,24},{24,32},{32,40},{40,48},{48,56},{56,64},{64,7... | collective-permute-start | bytes 1179656 | tf_op jit(solution)/shard_map/ppermute | solution.py:12
Sparse Core Ops, SparseCore 0:
  12.7 80.1 all-gather.3
  95.6 140.7 all-gather.5
where the time goes:
time: 267 us
  waiting for transfers between devices  217 us (81%)
  between operations  14.1 us (5%)
  local copies, waits for them, and re-layouts  12.3 us (5%)
  other arithmetic  9.98 us (4%)
  matrix products  7.76 us (3%)
  starting transfers between devices  5.51 us (2%)
    all_gather x1, waiting for transfers between devices, local(): whole = lax.all_gather(stale_kv[0], 'patch', axis=1, tiled=True)  110 us
    all_gather x1, waiting for transfers between devices, local(): lax.all_gather(normed, 'patch', axis=0, tiled=True)  78 us
    all_to_all x1, waiting for transfers between devices, local(): lax.all_to_all(columns, 'patch', split_axis=0, concat_axis=1, tiled=True)  21.3 us
    ppermute x1, waiting for transfers between devices, from_behind(): lax.ppermute(shard, axis, [(i, (i + by) % count) for i in range(count)])  7.2 us
    all_to_all x1, starting transfers between devices, local(): lax.all_to_all(columns, 'patch', split_axis=0, concat_axis=1, tiled=True)  5.36 us
  transfers between devices with their start and end apart: 4, of which 4 were waited for; matrix products, arithmetic and copies ran while one was open for 4% of the time, Pallas kernels for 0%

commit v1 on v0

--- a/solution.py
+++ b/solution.py
@@ -50,7 +50,9 @@
     values_new = qkv[:, 2 * width :]
     fresh = jnp.stack([keys_new, values_new])
     own_start = lax.axis_index("patch") * rows
-    whole = lax.all_gather(stale_kv[0], "patch", axis=1, tiled=True)
+    whole = jnp.concatenate(
+        lax.all_to_all(jnp.stack([stale_kv[0]] * lax.axis_size("patch")), "patch", 0, 0), axis=1
+    )
     whole = lax.dynamic_update_slice_in_dim(whole, fresh, own_start, 1)
     summed, top, total = partial_attention(queries, whole[0], whole[1])
     attended = (summed.reshape(rows, HEADS, HEAD_DIM) / total[..., None]).reshape(rows, width)

time: 267 us -> 231 us (0.87)
  the two profiles are of different devices: /device:TPU:2 before, /device:TPU:32 now
where the time goes in v1:
time: 231 us; the launch traced here: 230 us
  waiting for transfers between devices  174 us (75%)
  local copies, waits for them, and re-layouts  18.1 us (8%)
  between operations  14.2 us (6%)
  starting transfers between devices  8.49 us (4%)
  other arithmetic  8.07 us (3%)
  matrix products  7.76 us (3%)
    all_gather x1, waiting for transfers between devices, local(): lax.all_gather(normed, 'patch', axis=0, tiled=True)  81.3 us
    all_to_all x1, waiting for transfers between devices, local(): lax.all_to_all(jnp.stack([stale_kv[0]] * lax.axis_size('patch')), 'patch'...  70.1 us
    all_to_all x1, waiting for transfers between devices, local(): lax.all_to_all(columns, 'patch', split_axis=0, concat_axis=1, tiled=True)  14.9 us
    ppermute x1, waiting for transfers between devices, from_behind(): lax.ppermute(shard, axis, [(i, (i + by) % count) for i in range(count)])  7.24 us
    another operation x1, local copies, waits for them, and re-layouts, local(): jnp.stack([stale_kv[0]] * lax.axis_size('patch'))  5 us
    all_to_all x1, starting transfers between devices, local(): lax.all_to_all(jnp.stack([stale_kv[0]] * lax.axis_size('patch')), 'patch'...  4.87 us
  transfers between devices with their start and end apart: 4, of which 4 were waited for; matrix products, arithmetic and copies ran while one was open for 2% of the time, Pallas kernels for 0%

profile of v1, /device:TPU:32, one launch (start us, length us, event | category | flops | bytes accessed | tf_op | source)
XLA Modules:
  0.0 230.2 jit_solution(3865955121033562802)
XLA Ops:
  7.2 0.0 copy-start
  7.2 0.0 all-gather.2.cloned.1.call-start
  7.2 0.8 reduce.1
  8.1 0.7 reduce.2
  8.8 1.2 fusion.23
  9.9 0.7 convert_bitcast_fusion.1
  10.6 2.0 fusion.26
  12.6 0.0 all-gather.2.cloned.1.call-update
  12.6 81.3 %all-gather.2.cloned.1.call-done = bf16[1024,1536]{1,0:T(8,128)(2,1)} async-done(((bf16[128,1536]{1,0:T(8,128)(2,1)}), bf16[1024,1536]{1,0:T(8,128)(2,1)}) %all-gather.2.cloned.1.call-update) | async-done | bytes 3145744 | tf_op jit(solution)/shard_map/all_gather | solution.py:43
  94.0 0.0 copy-done
  94.0 3.9 %fusion.12 = bf16[72,8,8,128]{3,2,1,0:T(8,128)(2,1)S(1)} fusion(bf16[1024,1536]{1,0:T(8,128)(2,1)} %all-gather.2.cloned.1.call-done, bf16[1,1536,576]{1,2,0:T(8,128)(2,1)S(1)} %copy-done), kind=kOutput, calls=%fused_computation.12 | convolution fusion | flops 1812529152 | bytes 6094848 | tf_op jit(solution)/shard_map/dot_general | solution.py:42
  97.9 1.2 copy.36
  99.1 3.6 %all-to-all-start.1 = ((bf16[8,128,576]{1,2,0:T(8,128)(2,1)}), bf16[8,128,576]{1,2,0:T(8,128)(2,1)S(1)}, u32[]{:S(2)}, u32[]{:S(2)}) async-start(bf16[8,128,576]{1,2,0:T(8,128)(2,1)} %bitcast.72), calls=%async_computation.1 | async-start | bytes 2359296 | tf_op jit(solution)/shard_map/all_to_all | solution.py:47
  102.7 2.3 copy.21
  105.0 14.9 %all-to-all-done.1 = bf16[8,128,576]{1,2,0:T(8,128)(2,1)S(1)} async-done(((bf16[8,128,576]{1,2,0:T(8,128)(2,1)}), bf16[8,128,576]{1,2,0:T(8,128)(2,1)S(1)}, u32[]{:S(2)}, u32[]{:S(2)}) %all-to-all-start.1) | async-done | bytes 1179680 | tf_op jit(solution)/shard_map/all_to_all | solution.py:47
  119.8 5.0 %stack.12 = bf16[8,2,128,1536]{2,3,1,0:T(8,128)(2,1)} broadcast(bf16[2,128,1536]{1,2,0:T(8,128)(2,1)} %copy.21), dimensions={1,2,3} | broadcast | bytes 7077888 | tf_op jit(solution)/shard_map/stack | solution.py:54
  124.8 0.0 copy-start.4
  124.8 4.9 %all-to-all-start = ((bf16[8,2,128,1536]{2,3,1,0:T(8,128)(2,1)}), bf16[8,2,128,1536]{2,3,1,0:T(8,128)(2,1)}, u32[]{:S(2)}, u32[]{:S(2)}) async-start(bf16[8,2,128,1536]{2,3,1,0:T(8,128)(2,1)} %stack.12), calls=%async_computation | async-start | bytes 12582912 | tf_op jit(solution)/shard_map/all_to_all | solution.py:54
  129.7 0.0 copy-done.4
  129.8 1.0 fusion.32
  130.7 0.0 copy-start.2
  130.7 70.1 %all-to-all-done = bf16[8,2,128,1536]{2,3,1,0:T(8,128)(2,1)} async-done(((bf16[8,2,128,1536]{2,3,1,0:T(8,128)(2,1)}), bf16[8,2,128,1536]{2,3,1,0:T(8,128)(2,1)}, u32[]{:S(2)}, u32[]{:S(2)}) %all-to-all-start) | async-done | bytes 6291488 | tf_op jit(solution)/shard_map/all_to_all | solution.py:54
  200.8 0.0 copy-start.3
  200.8 3.7 %copy_bitcast_fusion = bf16[2,1024,1536]{1,2,0:T(8,128)(2,1)S(1)} fusion(bf16[8,2,128,1536]{2,3,1,0:T(8,128)(2,1)} %all-to-all-done), kind=kLoop, calls=%fused_computation | loop fusion | bytes 12582912 | tf_op jit(solution)/shard_map/reshape | solution.py:53
  204.6 0.0 copy-done.2
  204.6 0.0 copy-done.3
  204.6 0.4 fusion.28
  205.0 0.7 fusion.31
  205.7 1.3 bitcast_reduce_fusion
  207.0 1.0 fusion.1
  208.1 0.0 copy-start.1
  208.1 2.6 %fusion.20 = f32[128,12,128]{0,2,1:T(8,128)} fusion(bf16[1024,12,128]{0,2,1:T(8,128)(2,1)S(1)} %bitcast.73, f32[12,1024,128]{2,1,0:T(8,128)S(1)} %get-tuple-element.14, f32[128,12]{0,1:T(8,128)S(1)} %get-tuple-element.13, f32[128,12]{0,1:T(8,128)S(1)} %fusion.1), kind=kOutput, calls=%fused_computation.19 | convolution fusion | flops 407568384 | bytes 10235904 | tf_op jit(solution)/shard_map/nht,thd->nhd/dot_general | solution.py:27
  210.6 2.3 copy.27
  212.9 0.0 copy-done.1
  212.9 1.2 fusion.27
  214.2 0.0 collective-permute-start
  214.2 1.2 copy.28
  215.3 7.2 %collective-permute-done = bf16[1,128,1536]{2,1,0:T(8,128)(2,1)S(1)} collective-permute-done((bf16[1,128,1536]{2,1,0:T(8,128)(2,1)S(1)}, bf16[1,128,1536]{2,1,0:T(8,128)(2,1)S(1)}, u32[]{:S(2)}, u32[]{:S(2)}) %collective-permute-start) | collective-permute-done | bytes 393248 | tf_op jit(solution)/shard_map/ppermute | solution.py:12
  222.6 0.7 copy.39
  (2 shorter events, 0.0 us)
Async XLA Ops:
  7.2 86.8 %copy-start = (bf16[1,1536,576]{1,2,0:T(8,128)(2,1)S(1)}, bf16[1,1536,576]{1,2,0:T(8,128)(2,1)}, u32[]{:S(2)}) copy-start(bf16[1,1536,576]{1,2,0:T(8,128)(2,1)} %param.8) | copy-start | bytes 5308420
  7.2 86.8 %all-gather.2.cloned.1.call-start = ((), (), s32[]{:S(2)}) async-start(), calls=%async_computation.2 | async-start | bytes 3538944 | tf_op jit(solution)/shard_map/all_gather | solution.py:43
  99.1 20.7 %all-to-all-start.1 = ((bf16[8,128,576]{1,2,0:T(8,128)(2,1)}), bf16[8,128,576]{1,2,0:T(8,128)(2,1)S(1)}, u32[]{:S(2)}, u32[]{:S(2)}) async-start(bf16[8,128,576]{1,2,0:T(8,128)(2,1)} %bitcast.72), calls=%async_computation.1 | async-start | bytes 2359296 | tf_op jit(solution)/shard_map/all_to_all | solution.py:47
  124.8 4.9 %copy-start.4 = (f32[1,1536]{1,0:T(1,128)S(1)}, f32[1,1536]{1,0:T(1,128)}, u32[]{:S(2)}) copy-start(f32[1,1536]{1,0:T(1,128)} %param.11) | copy-start | bytes 18436
  124.8 76.0 %all-to-all-start = ((bf16[8,2,128,1536]{2,3,1,0:T(8,128)(2,1)}), bf16[8,2,128,1536]{2,3,1,0:T(8,128)(2,1)}, u32[]{:S(2)}, u32[]{:S(2)}) async-start(bf16[8,2,128,1536]{2,3,1,0:T(8,128)(2,1)} %stack.12), calls=%async_computation | async-start | bytes 12582912 | tf_op jit(solution)/shard_map/all_to_all | solution.py:54
  130.7 73.9 %copy-start.2 = (bf16[1,128,1536]{1,2,0:T(8,128)(2,1)S(1)}, bf16[1,128,1536]{1,2,0:T(8,128)(2,1)}, u32[]{:S(2)}) copy-start(bf16[1,128,1536]{1,2,0:T(8,128)(2,1)} %get-tuple-element.9) | copy-start | bytes 1179652
  200.8 3.8 %copy-start.3 = (bf16[1,128,1536]{1,2,0:T(8,128)(2,1)S(1)}, bf16[1,128,1536]{1,2,0:T(8,128)(2,1)}, u32[]{:S(2)}) copy-start(bf16[1,128,1536]{1,2,0:T(8,128)(2,1)} %get-tuple-element.10) | copy-start | bytes 1179652
  208.1 4.9 %copy-start.1 = (bf16[1,128,1536]{2,1,0:T(8,128)(2,1)S(1)}, bf16[1,128,1536]{2,1,0:T(8,128)(2,1)}, u32[]{:S(2)}) copy-start(bf16[1,128,1536]{2,1,0:T(8,128)(2,1)} %param.7) | copy-start | bytes 1179652
  214.2 8.4 %collective-permute-start = (bf16[1,128,1536]{2,1,0:T(8,128)(2,1)S(1)}, bf16[1,128,1536]{2,1,0:T(8,128)(2,1)S(1)}, u32[]{:S(2)}, u32[]{:S(2)}) collective-permute-start(bf16[1,128,1536]{2,1,0:T(8,128)(2,1)S(1)} %fusion.27), channel_id=1, source_target_pairs={{0,8},{8,16},{16,24},{24,32},{32,40},{40,48},{48,56},{56,64},{64,7... | collective-permute-start | bytes 1179656 | tf_op jit(solution)/shard_map/ppermute | solution.py:12
Sparse Core Ops, SparseCore 0:
  12.7 81.1 all-gather.1
